TPU v7x, 32 devices: a whole 2x2x4 slice. The times are simulated.
32 devices in a mesh: dir: 8 (over y, x, core), region: 4 (over z).
Axes of the slice: x: 2, y: 2, z: 4, core: 2. Of those that a mesh axis runs over, the one named last changes fastest.
Arguments:
- currents: bfloat16 [4, 48, 128, 256], P('region', 'dir'), may hold values from -6 to 6
- radiate: bfloat16 [1536, 128], replicated, may hold values from -0.5 to 0.5
- receive: bfloat16 [128, 1536], replicated, may hold values from -0.15625 to 0.15625
- transfer_table: bfloat16 [316, 1536], replicated, may hold values from -0.875 to 0.875
- near_blocks: bfloat16 [4, 48, 27, 128, 128], P('region', 'dir'), may hold values from -0.109375 to 0.109375
- dir_offsets: int32 [9], replicated, may hold values from 0 to 1536, as said below
- trans_src: int32 [4, 48, 48], P('region'), may hold values from -1 to 95, as said below
- trans_tid: int32 [4, 48, 48], P('region'), may hold values from 0 to 315
- near_src: int32 [4, 48, 27], P('region', 'dir'), may hold values from -1 to 71, as said below
Outputs:
- scattered: bfloat16 [4, 48, 128, 256], P('region', 'dir')
Inputs may be any that keep to these rules, and one draw needn't show every extreme that they name: dir_offsets starts at 0, ends at 1536 and rises; every band holds 96 to 288 direction samples, and some band holds exactly 288. `trans_src`: in each box's list the non-empty slots come first and name distinct boxes; a list holds 24 to 48 of them, and some list is full. `near_src`: each box's list starts with the box itself, then names distinct other boxes, then empty slots; a list holds 13 to 27 non-empty slots, and some list is full.
All inputs are finite; a program needn't handle non-finite values.
Results may differ from a plain program's by a relative error of at most 0.005.
Values may be sent and summed in bfloat16 or wider, within the bound.
No kernel may reach another device: no remote copies, remote signals or barrier semaphores. Data moves between devices by JAX's collectives and lax.ppermute only.
A program may use at most 192 MiB of HBM per device.

v0:
```python
import jax
import jax.numpy as jnp
from jax import lax
from jax.sharding import PartitionSpec as P


def padded(array, sides, width):
    for axis, dim in sides:
        devices, length = (lax.axis_size(axis), array.shape[dim])
        up = [(i, (i + 1) % devices) for i in range(devices - 1)]
        down = [(j, i) for i, j in up]
        last = lax.slice_in_dim(array, length - width, length, axis=dim)
        initial = lax.slice_in_dim(array, 0, width, axis=dim)
        before = lax.ppermute(last, axis, up)
        after = lax.ppermute(initial, axis, down)
        array = jnp.concatenate([before, array, after], axis=dim)
    return array


def band_weights(offsets, directions):
    dir_count = offsets.shape[0] - 1
    position = jnp.arange(directions, dtype=jnp.int32)
    starts = offsets[:-1]
    band_ends = offsets[1:]
    inside = (position[None, :] >= starts[:, None]) & (position[None, :] < band_ends[:, None])
    per_band = directions / (dir_count * (band_ends - starts).astype(jnp.float32))
    return jnp.sum(jnp.where(inside, per_band[:, None], jnp.zeros((), jnp.float32)), axis=0)


def shards(
    currents,
    radiate,
    receive,
    transfer_table,
    near_blocks,
    dir_offsets,
    trans_src,
    trans_tid,
    near_src,
):
    dir_count = lax.axis_size("dir")
    dir_index = lax.axis_index("dir")
    own_field = currents[0]
    box_count = own_field.shape[0]
    incidences = own_field.shape[2]
    directions = radiate.shape[0]
    classes = transfer_table.shape[0]
    zero_value = jnp.zeros((), jnp.bfloat16)
    weights = band_weights(dir_offsets, directions)
    recv_w = (receive.astype(jnp.float32) * weights[None, :]).astype(jnp.bfloat16)
    band_width = directions // dir_count + directions // (2 * dir_count)
    slot_index = lax.iota(jnp.int32, band_width)
    starts = dir_offsets[:-1]
    live_slots = slot_index[None, :] < (dir_offsets[1:] - starts)[:, None]
    pick_index = jnp.where(live_slots, starts[:, None] + slot_index[None, :], 0)
    flat_pick = pick_index.reshape(-1)
    flat_live = live_slots.reshape(-1)
    rad_used = jnp.where(flat_live[:, None], jnp.take(radiate, flat_pick, axis=0), zero_value)
    recv_used = jnp.where(flat_live[None, :], jnp.take(recv_w, flat_pick, axis=1), zero_value)
    own_picks = pick_index[dir_index]
    own_live = live_slots[dir_index]
    coef_used = jnp.where(
        own_live[None, :], jnp.take(transfer_table, own_picks, axis=1), zero_value
    )
    region_count = box_count * dir_count
    region_field = lax.all_gather(own_field, "dir", axis=0, tiled=True)
    wide_field = padded(region_field, (("region", 0),), region_count // 2)
    rad_own = lax.dynamic_slice_in_dim(rad_used, dir_index * band_width, band_width, 0)
    extended = jnp.einsum(
        "kq,sqr->skr", rad_own, wide_field, preferred_element_type=jnp.float32
    ).astype(jnp.bfloat16)
    inner_start = region_count // 2 - region_count // 4
    near_ext = wide_field[inner_start : inner_start + region_count + 2 * (region_count // 4)]
    ext_span = extended.shape[0]
    sources = trans_src[0]
    source_hot = (sources[:, :, None] == lax.iota(jnp.int32, ext_span)[None, None, :]).astype(
        jnp.bfloat16
    )
    class_hot = (trans_tid[0][:, :, None] == lax.iota(jnp.int32, classes)[None, None, :]).astype(
        jnp.bfloat16
    )
    pair_hot = jnp.einsum(
        "jls,jln->jsn", source_hot, class_hot, preferred_element_type=jnp.float32
    ).astype(jnp.bfloat16)
    matrix = jnp.einsum(
        "jsn,nt->tjs", pair_hot, coef_used, preferred_element_type=jnp.float32
    ).astype(jnp.bfloat16)
    translated = jnp.einsum(
        "tjs,str->jtr", matrix, extended, preferred_element_type=jnp.float32
    ).astype(jnp.bfloat16)
    translated = translated.reshape(dir_count, box_count, 1, band_width, incidences)
    returned = lax.all_to_all(translated, "dir", split_axis=0, concat_axis=2, tiled=True)
    returned = returned.reshape(box_count, dir_count * band_width, incidences)
    far_field = jnp.einsum("qc,bcr->bqr", recv_used, returned, preferred_element_type=jnp.float32)
    near_here = near_src[0]
    picked = jnp.take(near_ext, jnp.maximum(near_here, 0), axis=0)
    picked = jnp.where((near_here >= 0)[:, :, None, None], picked, zero_value)
    near_field = jnp.einsum(
        "bmpq,bmqr->bpr", near_blocks[0], picked, preferred_element_type=jnp.float32
    )
    return (far_field + near_field).astype(jnp.bfloat16)[None]


def solution(mesh):
    placed = (
        P("region", "dir", None, None),
        P(),
        P(),
        P(),
        P("region", "dir", None, None, None),
        P(),
        P("region", None, None),
        P("region", None, None),
        P("region", "dir", None),
    )
    return jax.shard_map(
        shards,
        mesh=mesh,
        in_specs=placed,
        out_specs=P("region", "dir", None, None),
        check_vma=False,
    )
```

profile of v0, /device:TPU:0, one launch (start us, length us, event | category | flops | bytes accessed | tf_op | source)
XLA Modules:
  0.0 234.0 jit_solution(11373164587903704093)
XLA Ops:
  6.5 0.7 all-gather.3.cloned.1.call-update
  7.3 1.4 fusion.84
  8.6 35.7 %all-gather.3.cloned.1.call-done = bf16[1,48,128,256]{3,2,0,1:T(8,128)(2,1)} async-done(((bf16[1,6,128,256]{3,2,0,1:T(8,128)(2,1)}), bf16[1,48,128,256]{3,2,0,1:T(8,128)(2,1)}) %all-gather.3.cloned.1.call-update) | async-done | bytes 3145744 | tf_op jit(solution)/shard_map/all_gather | solution.py:66
  44.3 4.0 %slice_bitcast_fusion.1 = (bf16[24,128,256]{2,1,0:T(8,128)(2,1)}, bf16[24,128,256]{2,1,0:T(8,128)(2,1)}) fusion(bf16[1,48,128,256]{3,2,1,0:T(8,128)(2,1)} %bitcast.65), kind=kLoop, calls=%fused_computation.30 | loop fusion | bytes 6291456 | tf_op jit(solution)/shard_map/slice | solution.py:12
  48.3 4.6 %collective-permute-start = (bf16[24,128,256]{2,1,0:T(8,128)(2,1)}, bf16[24,128,256]{2,1,0:T(8,128)(2,1)}, u32[]{:S(2)}, u32[]{:S(2)}) collective-permute-start(bf16[24,128,256]{2,1,0:T(8,128)(2,1)} %get-tuple-element.7), channel_id=1, source_target_pairs={{0,1},{1,2},{2,3},{4,5},{5,6},{6,7},{8,9},{9,10},{10,11},{12,13},{... | collective-permute-start | bytes 4718600 | tf_op jit(solution)/shard_map/ppermute | solution.py:14
  52.9 1.3 collective-permute-start.1
  55.1 0.7 dynamic-slice.1
  55.8 0.7 dynamic-slice
  56.6 1.4 copy.38
  58.1 5.6 %gather_fusion = bf16[2304,128]{1,0:T(8,128)(2,1)} fusion(bf16[1536,128]{1,0:T(8,128)(2,1)S(1)} %copy-done, s32[3072]{0:T(1024)S(1)} %pad_clamp_fusion), kind=kCustom, calls=%fused_computation | custom fusion | bytes 1188864 | tf_op jit(solution)/shard_map/jit(_take)/gather | solution.py:58
  63.6 0.9 fusion.72
  64.5 3.4 %gather_fusion.1 = bf16[288,316]{1,0:T(8,128)(2,1)S(1)} fusion(bf16[316,1536]{0,1:T(8,128)(2,1)} %copy.38, s32[1024]{0:T(1024)S(1)} %pad_clamp_fusion.2), kind=kCustom, calls=%fused_computation.1 | custom fusion | bytes 365184 | tf_op jit(solution)/shard_map/jit(_take)/gather | solution.py:63
  67.9 0.7 fusion.74
  68.7 6.1 %fusion.21 = bf16[288,48,96]{2,0,1:T(8,128)(2,1)} fusion(s32[48,48]{1,0:T(8,128)} %bitcast.70, s32[48,48]{1,0:T(8,128)} %bitcast.71, bf16[288,316]{1,0:T(8,128)(2,1)S(1)} %gather_fusion.1, pred[288]{0:T(512)(128)(4,1)S(1)} %dynamic-slice_reduce_fusion, pred[288]{0:T(512)(128)(4,1)S(1)} %compare_and_fusion.1), kind=kOutput, calls=%fused_computation.27 | convolution fusion | flops 982432512 | bytes 2855232 | tf_op jit(solution)/shard_map/jsn,nt->tjs/dot_general | solution.py:85
  74.8 11.3 %collective-permute-done = bf16[24,128,256]{2,1,0:T(8,128)(2,1)} collective-permute-done((bf16[24,128,256]{2,1,0:T(8,128)(2,1)}, bf16[24,128,256]{2,1,0:T(8,128)(2,1)}, u32[]{:S(2)}, u32[]{:S(2)}) %collective-permute-start) | collective-permute-done | bytes 1572896 | tf_op jit(solution)/shard_map/ppermute | solution.py:14
  86.1 5.3 %collective-permute-done.1 = bf16[24,128,256]{2,1,0:T(8,128)(2,1)} collective-permute-done((bf16[24,128,256]{2,1,0:T(8,128)(2,1)}, bf16[24,128,256]{2,1,0:T(8,128)(2,1)}, u32[]{:S(2)}, u32[]{:S(2)}) %collective-permute-start.1) | collective-permute-done | bytes 1572896 | tf_op jit(solution)/shard_map/ppermute | solution.py:15
  91.3 8.5 %convert_bitcast_fusion = bf16[96,288,256]{2,1,0:T(8,128)(2,1)} fusion(bf16[24,128,256]{2,1,0:T(8,128)(2,1)} %collective-permute-done.1, bf16[48,128,256]{2,1,0:T(8,128)(2,1)S(1)} %bitcast.66, bf16[24,128,256]{2,1,0:T(8,128)(2,1)} %collective-permute-done, bf16[2304,128]{1,0:T(8,128)(2,1)} %gather_fusion, s32[]{:T(128)S(6)} %select_n.106, ...), kind=kOutput, calls=%fused_computation.6 | convolution fusion | flops 1837965312 | bytes 20521540 | tf_op jit(solution)/shard_map/kq,sqr->skr/dot_general | solution.py:69
  99.9 17.8 %convert_bitcast_fusion.1 = bf16[48,288,256]{2,0,1:T(8,128)(2,1)} fusion(bf16[96,288,256]{2,1,0:T(8,128)(2,1)} %convert_bitcast_fusion, bf16[288,48,96]{2,0,1:T(8,128)(2,1)} %fusion.21), kind=kOutput, calls=%fused_computation.12 | convolution fusion | flops 683016192 | bytes 23887872 | tf_op jit(solution)/shard_map/tjs,str->jtr/dot_general | solution.py:88
  117.6 8.5 %copy.41 = bf16[48,288,256]{2,1,0:T(8,128)(2,1)} copy(bf16[48,288,256]{2,0,1:T(8,128)(2,1)} %convert_bitcast_fusion.1) | data formatting | bytes 14155776 | tf_op jit(solution)/shard_map/convert_element_type | solution.py:90
  126.1 5.2 %all-to-all-start = ((bf16[8,6,1,288,256]{4,3,1,2,0:T(8,128)(2,1)}), bf16[8,6,1,288,256]{4,3,1,2,0:T(8,128)(2,1)}, u32[]{:S(2)}, u32[]{:S(2)}) async-start(bf16[8,6,1,288,256]{4,3,1,2,0:T(8,128)(2,1)} %bitcast.64), calls=%async_computation | async-start | bytes 14155776 | tf_op jit(solution)/shard_map/all_to_all | solution.py:92
  131.3 0.9 copy.44
  132.2 0.8 select_reduce_fusion
  133.0 1.3 multiply_convert_fusion
  134.3 5.6 %gather_fusion.2 = bf16[2304,128]{1,0:T(8,128)(2,1)} fusion(bf16[128,1536]{0,1:T(8,128)(2,1)S(1)} %multiply_convert_fusion, s32[3072]{0:T(1024)S(1)} %pad_clamp_fusion), kind=kCustom, calls=%fused_computation.2 | custom fusion | bytes 1188864 | tf_op jit(solution)/shard_map/jit(_take)/gather | solution.py:59
  140.0 3.6 %pad_maximum_fusion = bf16[72,128,256]{2,1,0:T(8,128)(2,1)} fusion(bf16[24,128,256]{2,1,0:T(8,128)(2,1)} %collective-permute-done.1, bf16[48,128,256]{2,1,0:T(8,128)(2,1)S(1)} %bitcast.67, bf16[24,128,256]{2,1,0:T(8,128)(2,1)} %collective-permute-done), kind=kLoop, calls=%fused_computation.21 | loop fusion | flops 4718592 | bytes 11010048 | tf_op jit(solution)/shard_map/slice | solution.py:73
  143.6 9.9 %gather_fusion.3 = bf16[162,128,256]{2,1,0:T(8,128)(2,1)} fusion(bf16[72,128,256]{2,1,0:T(8,128)(2,1)} %pad_maximum_fusion, s32[1024]{0:T(1024)S(1)} %pad_clamp_fusion.1), kind=kCustom, calls=%fused_computation.3 | custom fusion | bytes 21234312 | tf_op jit(solution)/shard_map/jit(_take)/gather | solution.py:96
  153.4 13.8 %copy.46 = bf16[6,27,128,256]{2,3,1,0:T(8,128)(2,1)} copy(bf16[6,27,128,256]{3,2,1,0:T(8,128)(2,1)} %bitcast.63) | data formatting | bytes 21233664 | tf_op jit(solution)/shard_map/jit(_take)/gather | solution.py:96
  167.3 44.0 %all-to-all-done = bf16[8,6,1,288,256]{4,3,1,2,0:T(8,128)(2,1)} async-done(((bf16[8,6,1,288,256]{4,3,1,2,0:T(8,128)(2,1)}), bf16[8,6,1,288,256]{4,3,1,2,0:T(8,128)(2,1)}, u32[]{:S(2)}, u32[]{:S(2)}) %all-to-all-start) | async-done | bytes 7077920 | tf_op jit(solution)/shard_map/all_to_all | solution.py:92
  211.3 3.6 %copy.43 = bf16[8,6,1,288,256]{4,3,0,1,2:T(8,128)(2,1)S(1)} copy(bf16[8,6,1,288,256]{4,3,1,2,0:T(8,128)(2,1)} %all-to-all-done) | data formatting | bytes 14155776 | tf_op jit(solution)/shard_map/all_to_all | solution.py:92
  214.9 2.7 %fusion.46 = f32[6,256,128]{2,1,0:T(8,128)S(1)} fusion(bf16[6,2304,256]{2,1,0:T(8,128)(2,1)S(1)} %bitcast.68, bf16[2304,128]{1,0:T(8,128)(2,1)S(1)} %copy-done.4, pred[2304]{0:T(1024)(128)(4,1)S(1)} %copy-done.13, pred[2304]{0:T(1024)(128)(4,1)S(1)} %copy-done.8), kind=kOutput, calls=%fused_computation.37 | convolution fusion | flops 906559488 | bytes 8458752 | tf_op jit(solution)/shard_map/qc,bcr->bqr/dot_general | solution.py:94
  217.7 8.6 %fusion.41 = bf16[1,6,128,256]{2,3,1,0:T(8,128)(2,1)S(1)} fusion(f32[6,256,128]{2,1,0:T(8,128)S(1)} %fusion.46, bf16[1,6,27,128,128]{4,3,2,1,0:T(8,128)(2,1)} %param.13, bf16[6,27,128,256]{2,3,1,0:T(8,128)(2,1)} %copy.46, pred[6,27]{1,0:T(8,128)(4,1)S(1)} %get-tuple-element.15, pred[6,27]{1,0:T(8,128)(4,1)S(1)} %get-tuple-element.16), kind=kOutput, calls=%fused_computation.34 | convolution fusion | flops 1369964544 | bytes 17105220 | tf_op jit(solution)/shard_map/bmpq,bmqr->bpr/dot_general | solution.py:98
  226.2 0.9 copy.47
  (50 shorter events, 1.3 us)
Async XLA Ops:
  6.5 51.5 %copy-start = (bf16[1536,128]{1,0:T(8,128)(2,1)S(1)}, bf16[1536,128]{1,0:T(8,128)(2,1)}, u32[]{:S(2)}) copy-start(bf16[1536,128]{1,0:T(8,128)(2,1)} %param.10) | copy-start | bytes 1179652
  6.5 47.6 %copy-start.10 = (s32[9]{0:T(128)S(1)}, s32[9]{0:T(128)}, u32[]{:S(2)}) copy-start(s32[9]{0:T(128)} %param.14) | copy-start | bytes 112
  6.5 50.0 %copy-start.3 = (bf16[316,1536]{1,0:T(8,128)(2,1)S(1)}, bf16[316,1536]{1,0:T(8,128)(2,1)}, u32[]{:S(2)}) copy-start(bf16[316,1536]{1,0:T(8,128)(2,1)} %param.12) | copy-start | bytes 2912260
  6.5 37.8 %all-gather.3.cloned.1.call-start = ((), (), s32[]{:S(2)}) async-start(), calls=%async_computation.1 | async-start | bytes 3538944 | tf_op jit(solution)/shard_map/all_gather | solution.py:66
  8.6 46.2 %copy-start.11 = (s32[8]{0:T(128)}, s32[8]{0:T(128)S(1)}, u32[]{:S(2)}) copy-start(s32[8]{0:T(128)S(1)} %get-tuple-element.12) | copy-start | bytes 100
  48.3 37.8 %collective-permute-start = (bf16[24,128,256]{2,1,0:T(8,128)(2,1)}, bf16[24,128,256]{2,1,0:T(8,128)(2,1)}, u32[]{:S(2)}, u32[]{:S(2)}) collective-permute-start(bf16[24,128,256]{2,1,0:T(8,128)(2,1)} %get-tuple-element.7), channel_id=1, source_target_pairs={{0,1},{1,2},{2,3},{4,5},{5,6},{6,7},{8,9},{9,10},{10,11},{12,13},{... | collective-permute-start | bytes 4718600 | tf_op jit(solution)/shard_map/ppermute | solution.py:14
  52.9 38.5 %collective-permute-start.1 = (bf16[24,128,256]{2,1,0:T(8,128)(2,1)}, bf16[24,128,256]{2,1,0:T(8,128)(2,1)}, u32[]{:S(2)}, u32[]{:S(2)}) collective-permute-start(bf16[24,128,256]{2,1,0:T(8,128)(2,1)} %get-tuple-element.8), channel_id=1, source_target_pairs={{1,0},{2,1},{3,2},{5,4},{6,5},{7,6},{9,8},{10,9},{11,10},{13,12},{... | collective-permute-start | bytes 4718600 | tf_op jit(solution)/shard_map/ppermute | solution.py:15
  54.9 3.2 %copy-start.6 = (s32[8,288]{1,0:T(8,128)}, s32[8,288]{1,0:T(8,128)S(1)}, u32[]{:S(2)}) copy-start(s32[8,288]{1,0:T(8,128)S(1)} %get-tuple-element.14) | copy-start | bytes 27652
  55.1 1.4 copy-start.7
  55.8 0.7 copy-start.12
  63.6 27.7 %copy-start.2 = (bf16[1,48,128,256]{3,2,0,1:T(8,128)(2,1)S(1)}, bf16[1,48,128,256]{3,2,0,1:T(8,128)(2,1)}, u32[]{:S(2)}) copy-start(bf16[1,48,128,256]{3,2,0,1:T(8,128)(2,1)} %all-gather.3.cloned.1.call-done) | copy-start | bytes 9437188
  63.6 27.7 %copy-start.14 = (pred[288]{0:T(512)(128)(4,1)S(1)}, pred[288]{0:T(512)(128)(4,1)}, u32[]{:S(2)}) copy-start(pred[288]{0:T(512)(128)(4,1)} %dynamic-slice.1) | copy-start | bytes 868
  63.6 27.7 %copy-start.15 = (pred[288]{0:T(512)(128)(4,1)S(1)}, pred[288]{0:T(512)(128)(4,1)}, u32[]{:S(2)}) copy-start(pred[288]{0:T(512)(128)(4,1)} %dynamic-slice) | copy-start | bytes 868
  126.1 5.2 %copy-start.5 = (bf16[128,1536]{1,0:T(8,128)(2,1)S(1)}, bf16[128,1536]{1,0:T(8,128)(2,1)}, u32[]{:S(2)}) copy-start(bf16[128,1536]{1,0:T(8,128)(2,1)} %param.11) | copy-start | bytes 1179652
  126.1 85.2 %all-to-all-start = ((bf16[8,6,1,288,256]{4,3,1,2,0:T(8,128)(2,1)}), bf16[8,6,1,288,256]{4,3,1,2,0:T(8,128)(2,1)}, u32[]{:S(2)}, u32[]{:S(2)}) async-start(bf16[8,6,1,288,256]{4,3,1,2,0:T(8,128)(2,1)} %bitcast.64), calls=%async_computation | async-start | bytes 14155776 | tf_op jit(solution)/shard_map/all_to_all | solution.py:92
  131.3 8.5 %copy-start.9 = (s32[1,6,27]{2,0,1:T(1,128)S(1)}, s32[1,6,27]{2,0,1:T(1,128)}, u32[]{:S(2)}) copy-start(s32[1,6,27]{2,0,1:T(1,128)} %param.17) | copy-start | bytes 1948
  167.3 47.6 %copy-start.4 = (bf16[2304,128]{1,0:T(8,128)(2,1)S(1)}, bf16[2304,128]{1,0:T(8,128)(2,1)}, u32[]{:S(2)}) copy-start(bf16[2304,128]{1,0:T(8,128)(2,1)} %gather_fusion.2) | copy-start | bytes 1769476
  167.3 47.6 %copy-start.8 = (pred[2304]{0:T(1024)(128)(4,1)S(1)}, pred[2304]{0:T(1024)(128)(4,1)}, u32[]{:S(2)}) copy-start(pred[2304]{0:T(1024)(128)(4,1)} %copy-done.7) | copy-start | bytes 6916
  167.3 47.6 %copy-start.13 = (pred[2304]{0:T(1024)(128)(4,1)S(1)}, pred[2304]{0:T(1024)(128)(4,1)}, u32[]{:S(2)}) copy-start(pred[2304]{0:T(1024)(128)(4,1)} %copy-done.12) | copy-start | bytes 6916
  217.7 9.5 %copy-start.1 = (bf16[1536,128]{1,0:T(8,128)(2,1)S(1)}, bf16[1536,128]{1,0:T(8,128)(2,1)}, u32[]{:S(2)}) copy-start(bf16[1536,128]{1,0:T(8,128)(2,1)} %param.10) | copy-start | bytes 1179652
Sparse Core Ops, SparseCore 0:
  9.2 35.0 all-gather.2
where the time goes:
time: 235 us; the launch traced here: 234 us
  waiting for transfers between devices  96.9 us (41%)
  local copies, waits for them, and re-layouts  61.4 us (26%)
  matrix products  43.7 us (19%)
  between operations  13.6 us (6%)
  starting transfers between devices  11 us (5%)
  other arithmetic  7.38 us (3%)
    all_to_all x1, waiting for transfers between devices, shards(): lax.all_to_all(translated, 'dir', split_axis=0, concat_axis=2, tiled=True)  44 us
    all_gather x1, waiting for transfers between devices, shards(): region_field = lax.all_gather(own_field, 'dir', axis=0, tiled=True)  35.7 us
    gather x2, local copies, waits for them, and re-layouts, shards(): picked = jnp.take(near_ext, jnp.maximum(near_here, 0), axis=0)  23.7 us
    dot_general x1, matrix products, shards(): jnp.einsum('tjs,str->jtr', matrix, extended, preferred_element_type=jnp.f...  17.8 us
    ppermute x1, waiting for transfers between devices, padded(): before = lax.ppermute(last, axis, up)  11.3 us
    dot_general x1, matrix products, shards(): jnp.einsum('bmpq,bmqr->bpr', near_blocks[0], picked, preferred_element_ty...  8.55 us
    dot_general x1, matrix products, shards(): jnp.einsum('kq,sqr->skr', rad_own, wide_field, preferred_element_type=jnp...  8.54 us
    convert_element_type x1, local copies, waits for them, and re-layouts, shards(): translated = jnp.einsum('tjs,str->jtr', matrix, extended, preferred_eleme...  8.46 us
  transfers between devices with their start and end apart: 4, of which 4 were waited for; matrix products, arithmetic and copies ran while one was open for 25% of the time, Pallas kernels for 0%

commit v1 on v0

v1 whole, which is shorter than its diff:
```python
import functools

import jax
import jax.numpy as jnp
from jax import lax
from jax.experimental import pallas as pl
from jax.experimental.pallas import tpu as pltpu
from jax.sharding import PartitionSpec as P

BF16, F32, I32 = jnp.bfloat16, jnp.float32, jnp.int32
NT_DIMS = (((1,), (1,)), ((), ()))
LANES = 128
ROWS = 8
UNROLL = 4
MIB = 2**20


def pad_to(size, tile):
    return -(-size // tile) * tile


def whole(memory_space):
    return pl.BlockSpec(memory_space=memory_space)


def index_kernel(classes, near_shift, boxes, src_ref, tid_ref, near_ref, cls_ref, near_map_ref, used_ref):
    first = lax.axis_index("dir") * boxes
    slots = src_ref.shape[2]
    near_slots = near_ref.shape[2]
    width = cls_ref.shape[1]
    used_width = used_ref.shape[1]
    ext_at = lax.broadcasted_iota(I32, (width, slots), 0)
    near_at = lax.broadcasted_iota(I32, (width, near_slots), 0)
    class_at = lax.broadcasted_iota(I32, (used_width, slots), 0)
    row_at = lax.broadcasted_iota(I32, (ROWS, slots), 0)
    near_row_at = lax.broadcasted_iota(I32, (ROWS, near_slots), 0)
    near_lane_at = lax.broadcasted_iota(I32, (ROWS, near_slots), 1)
    out_row = lax.broadcasted_iota(I32, (ROWS, width), 0)
    seen = jnp.zeros((used_width, slots), F32)
    cls = jnp.full((ROWS, width), classes, I32)
    near_map = jnp.full((ROWS, width), near_slots, I32)
    for j in range(boxes):
        src = src_ref[0, pl.ds(first + j, 1), :]
        tid = tid_ref[0, pl.ds(first + j, 1), :]
        seen = jnp.maximum(seen, jnp.where((class_at == tid) & (src >= 0), 1.0, 0.0))
        hot = jnp.where(ext_at == src, 1.0, 0.0).astype(BF16)
        parts = jnp.where(row_at == 0, tid // 16, jnp.where(row_at == 1, tid % 16, 1)).astype(F32).astype(BF16)
        found = lax.dot_general(parts, hot, NT_DIMS, preferred_element_type=F32).astype(I32)
        value = jnp.where(found[2:3] > 0, found[0:1] * 16 + found[1:2], classes)
        cls = jnp.where(out_row == j, value, cls)
        near = near_ref[0, j : j + 1, :]
        near_hot = jnp.where((near_at == near + near_shift) & (near >= 0), 1.0, 0.0).astype(BF16)
        near_parts = jnp.where(near_row_at == 0, near_lane_at, 1).astype(F32).astype(BF16)
        near_found = lax.dot_general(near_parts, near_hot, NT_DIMS, preferred_element_type=F32).astype(I32)
        near_value = jnp.where(near_found[1:2] > 0, near_found[0:1], near_slots)
        near_map = jnp.where(out_row == j, near_value, near_map)
    ones = jnp.ones((ROWS, slots), BF16)
    used_ref[...] = lax.dot_general(ones, seen.astype(BF16), NT_DIMS, preferred_element_type=F32).astype(I32)
    cls_ref[...] = cls
    near_map_ref[...] = near_map


def operator_kernel(low, high, dir_count, aliased, off_ref, used_ref, table_ref, recv_ref, rad_ref, *rest):
    if aliased:
        _, out_ref, rows_ref, weighted_ref, list_ref = rest
    else:
        out_ref, rows_ref, weighted_ref, list_ref = rest
    directions = recv_ref.shape[1]
    position = lax.broadcasted_iota(I32, (1, directions), 1)
    band_size = jnp.ones((1, directions), I32)
    for d in range(off_ref.shape[0] - 1):
        start, end = off_ref[d], off_ref[d + 1]
        band_size = jnp.where((position >= start) & (position < end), end - start, band_size)
    weight = directions / ((off_ref.shape[0] - 1) * band_size.astype(F32))
    weighted_ref[...] = (recv_ref[...].astype(F32) * weight).astype(BF16)
    rows_ref[...] = table_ref[low:high, :].astype(F32)
    if not aliased:
        out_ref[out_ref.shape[0] - 1] = jnp.zeros(out_ref.shape[1:], BF16)

    def note(n, count):
        list_ref[count] = n
        return count + (used_ref[0, n] > 0).astype(I32)

    count = lax.fori_loop(low, high, note, 0, unroll=8)
    for u in range(UNROLL):
        list_ref[count + u] = list_ref[jnp.maximum(count - 1, 0)]

    def step(i, carry):
        for u in range(UNROLL):
            n = list_ref[i * UNROLL + u]
            row = rows_ref[pl.ds(n - low, 1), :].astype(BF16)
            product = weighted_ref[...] * row
            out_ref[n] = jnp.dot(product, rad_ref[...], preferred_element_type=F32).astype(BF16)
        return carry

    lax.fori_loop(0, (count + UNROLL - 1) // UNROLL, step, 0)


def apply_kernel(places, boxes, halo, first_call, last_call, cls_ref, near_map_ref, t_ref, near_ref, *rest):
    source_refs = rest[: sum(len(parts) for _, _, parts in places)]
    rest = rest[len(source_refs) :]
    if not first_call:
        sum_ref, out_ref, *lhs_refs = rest
    else:
        out_ref, *lhs_refs = rest
    me = lax.axis_index("dir")
    region_boxes = boxes * lax.axis_size("dir")
    near_slots = near_ref.shape[2]
    size = near_ref.shape[3]
    total = None if first_call else sum_ref[...]
    at = 0
    for step, (rim, mask, parts) in enumerate(places):
        lhs_ref = lhs_refs[step % len(lhs_refs)]
        owner = me ^ mask
        if rim:
            upper = owner * boxes >= halo
            base = owner * boxes + jnp.where(upper, halo - region_boxes, halo + region_boxes)
        else:
            base = owner * boxes + halo
        for j in range(boxes):
            for b in range(boxes):
                n = cls_ref[j, base + b]
                m = near_map_ref[j, base + b]
                near = near_ref[0, j, jnp.minimum(m, near_slots - 1)]
                block = t_ref[n] + jnp.where(m < near_slots, near, jnp.zeros_like(near))
                lhs_ref[j * size : (j + 1) * size, b * size : (b + 1) * size] = block
        values = [ref[...] for ref in source_refs[at : at + len(parts)]]
        at += len(parts)
        rhs = values[0] if len(values) == 1 else jnp.concatenate(values, 0)
        rhs = rhs.reshape(boxes * size, rhs.shape[-1])
        added = jnp.dot(lhs_ref[...], rhs, preferred_element_type=F32)
        if step == 0 and first_call:
            out_ref[...] = added.reshape(out_ref.shape)
        elif step == 0:
            out_ref[...] = sum_ref[...] + added.reshape(out_ref.shape)
        else:
            out_ref[...] += added.reshape(out_ref.shape)


def shards(
    currents,
    radiate,
    receive,
    transfer_table,
    near_blocks,
    dir_offsets,
    trans_src,
    trans_tid,
    near_src,
):
    dir_count = lax.axis_size("dir")
    region_count = lax.axis_size("region")
    own = currents[0]
    boxes, unknowns, incidences = own.shape
    region_boxes = boxes * dir_count
    halo = region_boxes // 2
    near_halo = region_boxes // 4
    classes, directions = transfer_table.shape
    half = pad_to(classes // 2, 16)
    top = dir_count // 2
    inner = range(2, top, 2)
    split = boxes // 2

    def partner(array, mask):
        return lax.ppermute(array, "dir", [(i, i ^ mask) for i in range(dir_count)])

    along = []
    for i in range(dir_count):
        for z in range(region_count):
            target = z + 1 if i >= top else z - 1
            if 0 <= target < region_count:
                along.append((i * region_count + z, i * region_count + target))

    def beyond(array):
        return lax.ppermute(array, ("dir", "region"), along)

    width = pad_to(region_boxes + 2 * halo, LANES)
    used_width = pad_to(classes, LANES)
    cls, near_map, used = pl.pallas_call(
        functools.partial(index_kernel, classes, halo - near_halo, boxes),
        out_shape=(
            jax.ShapeDtypeStruct((ROWS, width), I32),
            jax.ShapeDtypeStruct((ROWS, width), I32),
            jax.ShapeDtypeStruct((ROWS, used_width), I32),
        ),
    )(trans_src, trans_tid, near_src)

    def operators(low, high, before):
        aliased = before is not None
        args = [dir_offsets, used, transfer_table, receive, radiate] + ([before] if aliased else [])
        specs = [whole(pltpu.SMEM), whole(pltpu.SMEM)] + [whole(pltpu.VMEM)] * (len(args) - 2)
        return pl.pallas_call(
            functools.partial(operator_kernel, low, high, dir_count, aliased),
            in_specs=specs,
            out_specs=whole(pltpu.VMEM),
            out_shape=pltpu.VMEM((classes + 1, unknowns, unknowns), BF16),
            input_output_aliases={5: 0} if aliased else {},
            scratch_shapes=[
                pltpu.VMEM((high - low, directions), F32),
                pltpu.VMEM((unknowns, directions), BF16),
                pltpu.SMEM((pad_to(high - low, 8) + 2 * UNROLL,), I32),
            ],
            compiler_params=pltpu.CompilerParams(vmem_limit_bytes=40 * MIB),
            cost_estimate=pl.CostEstimate(
                flops=classes * unknowns * unknowns * directions, bytes_accessed=MIB, transcendentals=0
            ),
        )(*args)

    def apply(places, total, last):
        parts = [part for _, _, group in places for part in group]
        args = [cls, near_map, table, near_blocks] + parts + ([] if total is None else [total])
        specs = [whole(pltpu.SMEM)] * 2 + [whole(pltpu.VMEM)] * (len(args) - 2)
        layout = [(rim, mask, [None] * len(group)) for rim, mask, group in places]
        shape = (boxes, unknowns, incidences)
        return pl.pallas_call(
            functools.partial(apply_kernel, layout, boxes, halo, total is None, last),
            in_specs=specs,
            out_specs=whole(pltpu.VMEM),
            out_shape=pltpu.VMEM(shape, F32),
            input_output_aliases={} if total is None else {len(args) - 1: 0},
            scratch_shapes=[pltpu.VMEM((boxes * unknowns, boxes * unknowns), BF16)] * 2,
            compiler_params=pltpu.CompilerParams(vmem_limit_bytes=48 * MIB),
            cost_estimate=pl.CostEstimate(
                flops=2 * len(places) * (boxes * unknowns) ** 2 * incidences, bytes_accessed=MIB, transcendentals=0
            ),
        )(*args)

    field = {0: own}
    rim = {}
    for m in inner:
        field[m] = partner(own, m)
    field[top] = partner(own, top)
    rim[0] = beyond(own)
    field[1] = partner(own, 1)
    table = operators(0, half, None)

    tied = lax.optimization_barrier((table, [field[m] for m in inner], field[top], rim[0]))
    table, inner_fields, field[top], rim[0] = tied
    for m, value in zip(inner, inner_fields):
        field[m] = value
    for m in inner:
        field[top + m] = partner(field[top], m)
    rim[top] = partner(rim[0], top)
    for m in inner:
        rim[m] = beyond(field[m])
    for m in inner:
        field[m + 1] = partner(field[m], 1)
    field[top + 1] = partner(field[top], 1)
    rim[1] = partner(rim[0], 1)
    table = operators(half, classes, table)
    early = [(False, m, [field[m]]) for m in (0, 1, *inner, *[m + 1 for m in inner], top, top + 1)]
    early += [(True, m, [rim[m]]) for m in (0, 1)]
    total = apply(early, None, False)

    tied = lax.optimization_barrier(
        (total, [field[top + m] for m in inner], [rim[m] for m in inner], rim[top])
    )
    total, far_fields, inner_rims, rim[top] = tied
    for m, value, other in zip(inner, far_fields, inner_rims):
        field[top + m], rim[m] = value, other
    last = {}
    for m in inner:
        last[m] = [partner(rim[top][:split], m), partner(rim[m][split:], top)]
    for m in inner:
        field[top + m + 1] = partner(field[top + m], 1)
        rim[m + 1] = partner(rim[m], 1)
    rim[top + 1] = partner(rim[top], 1)
    middle = [(False, top + m, [field[top + m]]) for m in inner]
    middle += [(True, m, [rim[m]]) for m in (*inner, top)]
    total = apply(middle, total, False)
    late = [(False, top + m + 1, [field[top + m + 1]]) for m in inner]
    late += [(True, m + 1, [rim[m + 1]]) for m in (*inner, top)]
    late += [(True, top + m, last[m]) for m in inner]
    late += [(True, top + m + 1, [partner(part, 1) for part in last[m]]) for m in inner]
    total = apply(late, total, True)
    return total.astype(BF16)[None]


def solution(mesh):
    placed = (
        P("region", "dir", None, None),
        P(),
        P(),
        P(),
        P("region", "dir", None, None, None),
        P(),
        P("region", None, None),
        P("region", None, None),
        P("region", "dir", None),
    )
    return jax.shard_map(
        shards,
        mesh=mesh,
        in_specs=placed,
        out_specs=P("region", "dir", None, None),
        check_vma=False,
    )
```

time: 235 us -> 91.7 us (0.39)
  waiting for transfers between devices: 96.9 us -> 6.35 us
  Pallas kernels: 0 us -> 57.1 us
  local copies, waits for them, and re-layouts: 61.4 us -> 10.6 us
  matrix products: 43.7 us -> 0 us
  between operations: 13.6 us -> 0.27 us
  other arithmetic: 7.38 us -> 0.79 us
  starting transfers between devices: 11 us -> 16 us
    pallas_call x0 -> x6, Pallas kernels: none -> 57.1 us  [the longest x3 27.8 us: apply(): pl.pallas_call(functools.partial(apply_kernel, layout, boxes, halo, total...]
    all_to_all x1 -> x0, waiting for transfers between devices: 44 us -> none  [shards(): lax.all_to_all(translated, 'dir', split_axis=0, concat_axis=2, tiled=True)]
    dot_general x5 -> x0, matrix products: 43.7 us -> none  [the longest x1 17.8 us: shards(): jnp.einsum('tjs,str->jtr', matrix, extended, preferred_element_type=jnp.f...]
    gather x5 -> x0, local copies, waits for them, and re-layouts: 38.2 us -> none  [the longest x2 23.7 us: shards(): picked = jnp.take(near_ext, jnp.maximum(near_here, 0), axis=0)]
    all_gather x1 -> x0, waiting for transfers between devices: 35.7 us -> none  [shards(): region_field = lax.all_gather(own_field, 'dir', axis=0, tiled=True)]
    ppermute x2 -> x17, waiting for transfers between devices: 16.6 us -> 6.35 us  [the longest x15 6.34 us: partner(): return lax.ppermute(array, 'dir', [(i, i ^ mask) for i in range(dir_count)])]
    ppermute x2 -> x17, starting transfers between devices: 5.84 us -> 16 us  [the longest x15 13.4 us: partner(): return lax.ppermute(array, 'dir', [(i, i ^ mask) for i in range(dir_count)])]
    convert_element_type x1 -> x0, local copies, waits for them, and re-layouts: 8.46 us -> none  [shards(): translated = jnp.einsum('tjs,str->jtr', matrix, extended, preferred_eleme...]
  transfers between devices with their start and end apart: 4 -> 17, of which waited for: 4 -> 2; matrix products, arithmetic and copies ran while one was open for 25% -> 1% of each run, Pallas kernels for 0% -> 53%
where the time goes in v1:
time: 91.7 us; the launch traced here: 91.1 us
  Pallas kernels  57.1 us (62%)
  starting transfers between devices  16 us (17%)
  local copies, waits for them, and re-layouts  10.6 us (12%)
  waiting for transfers between devices  6.35 us (7%)
    pallas_call x3, Pallas kernels, apply(): pl.pallas_call(functools.partial(apply_kernel, layout, boxes, halo, total...  27.8 us
    pallas_call x2, Pallas kernels, operators(): pl.pallas_call(functools.partial(operator_kernel, low, high, dir_count, a...  27.5 us
    ppermute x15, starting transfers between devices, partner(): return lax.ppermute(array, 'dir', [(i, i ^ mask) for i in range(dir_count)])  13.4 us
    unnamed x25, local copies, waits for them, and re-layouts  10.6 us
    ppermute x15, waiting for transfers between devices, partner(): return lax.ppermute(array, 'dir', [(i, i ^ mask) for i in range(dir_count)])  6.34 us
    ppermute x2, starting transfers between devices, beyond(): return lax.ppermute(array, ('dir', 'region'), along)  2.56 us
  transfers between devices with their start and end apart: 17, of which 2 were waited for; matrix products, arithmetic and copies ran while one was open for 1% of the time, Pallas kernels for 53%

profile of v1, /device:TPU:0, one launch (start us, length us, event | category | flops | bytes accessed | tf_op | source)
XLA Modules:
  0.0 91.1 jit_solution(12768337345427214993)
XLA Ops:
  0.0 2.9 %collective-permute-start = (bf16[6,128,256]{2,1,0:T(8,128)(2,1)}, bf16[6,128,256]{2,1,0:T(8,128)(2,1)S(1)}, u32[]{:S(2)}, u32[]{:S(2)}) collective-permute-start(bf16[6,128,256]{2,1,0:T(8,128)(2,1)} %bitcast.3), channel_id=1, source_target_pairs={{0,8},{4,12},{8,0},{12,4},{16,24},{20,28},{24,16},{28,20},{1,9},{5... | collective-permute-start | bytes 1179656 | tf_op jit(solution)/shard_map/ppermute | solution.py:165
  2.9 1.5 %collective-permute-start.1 = (bf16[6,128,256]{2,1,0:T(8,128)(2,1)}, bf16[6,128,256]{2,1,0:T(8,128)(2,1)S(1)}, u32[]{:S(2)}, u32[]{:S(2)}) collective-permute-start(bf16[6,128,256]{2,1,0:T(8,128)(2,1)} %bitcast.4), channel_id=1, source_target_pairs={{0,16},{4,20},{8,24},{12,28},{16,0},{20,4},{24,8},{28,12},{1,17},{... | collective-permute-start | bytes 1179656 | tf_op jit(solution)/shard_map/ppermute | solution.py:165
  4.5 1.3 %collective-permute-start.2 = (bf16[6,128,256]{2,1,0:T(8,128)(2,1)}, bf16[6,128,256]{2,1,0:T(8,128)(2,1)S(1)}, u32[]{:S(2)}, u32[]{:S(2)}) collective-permute-start(bf16[6,128,256]{2,1,0:T(8,128)(2,1)} %bitcast.5), channel_id=1, source_target_pairs={{1,0},{2,1},{3,2},{5,4},{6,5},{7,6},{9,8},{10,9},{11,10},{13,12},{... | collective-permute-start | bytes 1179656 | tf_op jit(solution)/shard_map/ppermute | solution.py:175
  5.7 0.1 collective-permute-start.3
  5.8 1.3 %copy.13.near_ref = s32[1,6,27]{2,1,0:T(8,128)} copy(s32[1,6,27]{2,0,1:T(1,128)} %param.17) | data formatting | bytes 1296 | tf_op args[8]
  7.1 1.8 %shard_map.91 = (s32[8,128]{1,0:T(8,128)}, s32[8,128]{1,0:T(8,128)}, s32[8,384]{1,0:T(8,128)}) custom-call(s32[1,48,48]{2,1,0:T(8,128)} %src_ref.1, s32[1,48,48]{2,1,0:T(8,128)} %tid_ref.1, s32[1,6,27]{2,1,0:T(8,128)} %copy.13.near_ref), custom_call_target="tpu_custom_call" | custom-call | tf_op jit(solution)/shard_map/pallas_call | solution.py:179
  8.9 1.2 %copy-done.6 = bf16[316,1536]{1,0:T(8,128)(2,1)S(1)} copy-done((bf16[316,1536]{1,0:T(8,128)(2,1)S(1)}, bf16[316,1536]{1,0:T(8,128)(2,1)}, u32[]{:S(2)}) %copy-start.6) | copy-done | bytes 970776
  10.1 1.0 %copy-done.7 = bf16[128,1536]{1,0:T(8,128)(2,1)S(1)} copy-done((bf16[128,1536]{1,0:T(8,128)(2,1)S(1)}, bf16[128,1536]{1,0:T(8,128)(2,1)}, u32[]{:S(2)}) %copy-start.7) | copy-done | bytes 393240
  11.1 1.0 %copy-done.8 = bf16[1536,128]{1,0:T(8,128)(2,1)S(1)} copy-done((bf16[1536,128]{1,0:T(8,128)(2,1)S(1)}, bf16[1536,128]{1,0:T(8,128)(2,1)}, u32[]{:S(2)}) %copy-start.8) | copy-done | bytes 393240
  12.1 0.7 copy-done.10
  12.8 0.7 copy-done.11
  13.4 13.6 %shard_map.92.rest_0_ = bf16[317,128,128]{2,1,0:T(8,128)(2,1)S(1)} custom-call(s32[9]{0:T(128)S(1)} %copy-done.11, s32[8,384]{1,0:T(8,128)S(1)} %copy-done.10, bf16[316,1536]{1,0:T(8,128)(2,1)S(1)} %copy-done.6, bf16[128,1536]{1,0:T(8,128)(2,1)S(1)} %copy-done.7, bf16[1536,128]{1,0:T(8,128)(2,1)S(1)} %copy-done.8), custom_call_target="tpu_custom_call" | custom-call | flops 7952400384 | bytes 1048576 | tf_op jit(solution)/shard_map/pallas_call | solution.py:192
  27.1 0.1 collective-permute-start.4
  27.2 0.5 collective-permute-start.5
  27.7 0.5 collective-permute-start.7
  28.2 1.3 %collective-permute-start.8 = (bf16[6,128,256]{2,1,0:T(8,128)(2,1)S(1)}, bf16[6,128,256]{2,1,0:T(8,128)(2,1)S(1)}, u32[]{:S(2)}, u32[]{:S(2)}) collective-permute-start(bf16[6,128,256]{2,1,0:T(8,128)(2,1)S(1)} %collective-permute-done.rest_2_), channel_id=1, source_target_pairs={{1,0},{2,1},{3,2},{5,4},{6,5},{7,6},{9,8},{10,9},{11,10},{13,12},{... | collective-permute-start | bytes 1179656 | tf_op jit(solution)/shard_map/ppermute | solution.py:175
  29.5 0.7 copy-done.2
  30.3 5.6 %collective-permute-start.9 = (bf16[6,128,256]{2,1,0:T(8,128)(2,1)S(1)}, bf16[6,128,256]{2,1,0:T(8,128)(2,1)S(1)}, u32[]{:S(2)}, u32[]{:S(2)}) collective-permute-start(bf16[6,128,256]{2,1,0:T(8,128)(2,1)S(1)} %collective-permute-done.2.rest_6_), channel_id=1, source_target_pairs={{0,16},{4,20},{8,24},{12,28},{16,0},{20,4},{24,8},{28,12},{1,17},{... | collective-permute-start | bytes 1179656 | tf_op jit(solution)/shard_map/ppermute | solution.py:165
  35.9 13.9 %shard_map.93.t_ref = bf16[317,128,128]{2,1,0:T(8,128)(2,1)S(1)} custom-call(s32[9]{0:T(128)S(1)} %copy-done.11, s32[8,384]{1,0:T(8,128)S(1)} %copy-done.10, bf16[316,1536]{1,0:T(8,128)(2,1)S(1)} %copy-done.6, bf16[128,1536]{1,0:T(8,128)(2,1)S(1)} %copy-done.7, bf16[1536,128]{1,0:T(8,128)(2,1)S(1)} %copy-done.9, ...), custom_call_target="tpu_custom_call", output_to_operand_aliasing={{}: (5, {})} | custom-call | flops 7952400384 | bytes 1048576 | tf_op jit(solution)/shard_map/pallas_call | solution.py:192
  49.8 4.0 %copy-done = bf16[317,128,128]{2,1,0:T(8,128)(2,1)} copy-done((bf16[317,128,128]{2,1,0:T(8,128)(2,1)}, bf16[317,128,128]{2,1,0:T(8,128)(2,1)S(1)}, u32[]{:S(2)}) %copy-start) | copy-done | bytes 10387480
  53.8 11.2 %shard_map.94.rest_3_ = f32[6,128,256]{2,1,0:T(8,128)S(1)} custom-call(s32[8,128]{1,0:T(8,128)S(1)} %copy-done.4, s32[8,128]{1,0:T(8,128)S(1)} %copy-done.5, bf16[317,128,128]{2,1,0:T(8,128)(2,1)} %copy-done, bf16[1,6,27,128,128]{4,3,2,1,0:T(8,128)(2,1)} %near_ref.6, bf16[6,128,256]{2,1,0:T(8,128)(2,1)S(1)} %bitcast.7, bf16[6,128,256]{2,1,0:T(8,128)(2,1)S(1)} %copy-done.3, ...), custom_call_target="tpu_custom_call" | custom-call | flops 2415919104 | bytes 1048576 | tf_op jit(solution)/shard_map/pallas_call | solution.py:215
  65.1 0.1 collective-permute-start.12
  65.2 0.6 collective-permute-start.10
  65.8 0.1 collective-permute-start.11
  65.9 0.9 %collective-permute-start.13 = (bf16[3,128,256]{2,1,0:T(8,128)(2,1)S(1)}, bf16[3,128,256]{2,1,0:T(8,128)(2,1)S(1)}, u32[]{:S(2)}, u32[]{:S(2)}) collective-permute-start(bf16[3,128,256]{2,1,0:T(8,128)(2,1)S(1)} %slice.6), channel_id=1, source_target_pairs={{0,8},{4,12},{8,0},{12,4},{16,24},{20,28},{24,16},{28,20},{1,9},{5... | collective-permute-start | bytes 589832 | tf_op jit(solution)/shard_map/ppermute | solution.py:165
  66.8 0.4 collective-permute-start.14
  67.2 5.9 %collective-permute-done.13.rest_3_ = bf16[3,128,256]{2,1,0:T(8,128)(2,1)S(1)} collective-permute-done((bf16[3,128,256]{2,1,0:T(8,128)(2,1)S(1)}, bf16[3,128,256]{2,1,0:T(8,128)(2,1)S(1)}, u32[]{:S(2)}, u32[]{:S(2)}) %collective-permute-start.13) | collective-permute-done | bytes 196640 | tf_op jit(solution)/shard_map/ppermute | solution.py:165
  73.1 0.4 collective-permute-done.14.rest_4_
  73.5 0.1 collective-permute-start.16
  73.6 7.4 %shard_map.95.rest_7_ = f32[6,128,256]{2,1,0:T(8,128)S(1)} custom-call(s32[8,128]{1,0:T(8,128)S(1)} %copy-done.4, s32[8,128]{1,0:T(8,128)S(1)} %copy-done.5, bf16[317,128,128]{2,1,0:T(8,128)(2,1)} %copy-done, bf16[1,6,27,128,128]{4,3,2,1,0:T(8,128)(2,1)} %near_ref.6, ...), custom_call_target="tpu_custom_call", output_to_operand_aliasing={{}: (7, {})} | custom-call | flops 905969664 | bytes 1048576 | tf_op jit(solution)/shard_map/pallas_call | solution.py:215
  81.1 9.2 %shard_map.96 = f32[6,128,256]{2,1,0:T(8,128)S(1)} custom-call(s32[8,128]{1,0:T(8,128)S(1)} %copy-done.4, s32[8,128]{1,0:T(8,128)S(1)} %copy-done.5, bf16[317,128,128]{2,1,0:T(8,128)(2,1)} %copy-done, bf16[1,6,27,128,128]{4,3,2,1,0:T(8,128)(2,1)} %near_ref.6, ...), custom_call_target="tpu_custom_call", output_to_operand_aliasing={{}: (11, {})} | custom-call | flops 1509949440 | bytes 1048576 | tf_op jit(solution)/shard_map/pallas_call | solution.py:215
  90.3 0.8 convert_bitcast_fusion
  (36 shorter events, 0.1 us)
Async XLA Ops:
  0.0 27.1 %collective-permute-start = (bf16[6,128,256]{2,1,0:T(8,128)(2,1)}, bf16[6,128,256]{2,1,0:T(8,128)(2,1)S(1)}, u32[]{:S(2)}, u32[]{:S(2)}) collective-permute-start(bf16[6,128,256]{2,1,0:T(8,128)(2,1)} %bitcast.3), channel_id=1, source_target_pairs={{0,8},{4,12},{8,0},{12,4},{16,24},{20,28},{24,16},{28,20},{1,9},{5... | collective-permute-start | bytes 1179656 | tf_op jit(solution)/shard_map/ppermute | solution.py:165
  2.9 24.2 %collective-permute-start.1 = (bf16[6,128,256]{2,1,0:T(8,128)(2,1)}, bf16[6,128,256]{2,1,0:T(8,128)(2,1)S(1)}, u32[]{:S(2)}, u32[]{:S(2)}) collective-permute-start(bf16[6,128,256]{2,1,0:T(8,128)(2,1)} %bitcast.4), channel_id=1, source_target_pairs={{0,16},{4,20},{8,24},{12,28},{16,0},{20,4},{24,8},{28,12},{1,17},{... | collective-permute-start | bytes 1179656 | tf_op jit(solution)/shard_map/ppermute | solution.py:165
  4.5 22.6 %collective-permute-start.2 = (bf16[6,128,256]{2,1,0:T(8,128)(2,1)}, bf16[6,128,256]{2,1,0:T(8,128)(2,1)S(1)}, u32[]{:S(2)}, u32[]{:S(2)}) collective-permute-start(bf16[6,128,256]{2,1,0:T(8,128)(2,1)} %bitcast.5), channel_id=1, source_target_pairs={{1,0},{2,1},{3,2},{5,4},{6,5},{7,6},{9,8},{10,9},{11,10},{13,12},{... | collective-permute-start | bytes 1179656 | tf_op jit(solution)/shard_map/ppermute | solution.py:175
  5.7 23.8 %collective-permute-start.3 = (bf16[6,128,256]{2,1,0:T(8,128)(2,1)}, bf16[6,128,256]{2,1,0:T(8,128)(2,1)S(1)}, u32[]{:S(2)}, u32[]{:S(2)}) collective-permute-start(bf16[6,128,256]{2,1,0:T(8,128)(2,1)} %bitcast.6), channel_id=1, source_target_pairs={{0,4},{4,0},{8,12},{12,8},{16,20},{20,16},{24,28},{28,24},{1,5},{5... | collective-permute-start | bytes 1179656 | tf_op jit(solution)/shard_map/ppermute | solution.py:165
  8.9 1.2 %copy-start.6 = (bf16[316,1536]{1,0:T(8,128)(2,1)S(1)}, bf16[316,1536]{1,0:T(8,128)(2,1)}, u32[]{:S(2)}) copy-start(bf16[316,1536]{1,0:T(8,128)(2,1)} %table_ref.3) | copy-start | bytes 2912260
  10.1 1.0 %copy-start.7 = (bf16[128,1536]{1,0:T(8,128)(2,1)S(1)}, bf16[128,1536]{1,0:T(8,128)(2,1)}, u32[]{:S(2)}) copy-start(bf16[128,1536]{1,0:T(8,128)(2,1)} %recv_ref.3) | copy-start | bytes 1179652
  11.1 1.0 %copy-start.8 = (bf16[1536,128]{1,0:T(8,128)(2,1)S(1)}, bf16[1536,128]{1,0:T(8,128)(2,1)}, u32[]{:S(2)}) copy-start(bf16[1536,128]{1,0:T(8,128)(2,1)} %rad_ref.3) | copy-start | bytes 1179652
  12.1 0.7 copy-start.10
  12.8 0.7 copy-start.11
  13.4 22.5 %copy-start.9 = (bf16[1536,128]{1,0:T(8,128)(2,1)S(1)}, bf16[1536,128]{1,0:T(8,128)(2,1)}, u32[]{:S(2)}) copy-start(bf16[1536,128]{1,0:T(8,128)(2,1)} %rad_ref.3) | copy-start | bytes 1179652
  27.0 26.8 %copy-start.1 = (bf16[1,6,128,256]{3,2,1,0:T(8,128)(2,1)S(1)}, bf16[1,6,128,256]{3,2,1,0:T(8,128)(2,1)}, u32[]{:S(2)}) copy-start(bf16[1,6,128,256]{3,2,1,0:T(8,128)(2,1)} %param.9) | copy-start | bytes 1179652
  27.1 26.7 %copy-start.4 = (s32[8,128]{1,0:T(8,128)S(1)}, s32[8,128]{1,0:T(8,128)}, u32[]{:S(2)}) copy-start(s32[8,128]{1,0:T(8,128)} %get-tuple-element.16.cls_ref) | copy-start | bytes 12292
  27.1 26.7 %copy-start.5 = (s32[8,128]{1,0:T(8,128)S(1)}, s32[8,128]{1,0:T(8,128)}, u32[]{:S(2)}) copy-start(s32[8,128]{1,0:T(8,128)} %get-tuple-element.17.near_map_ref) | copy-start | bytes 12292
  27.1 3.2 %collective-permute-start.4 = (bf16[6,128,256]{2,1,0:T(8,128)(2,1)S(1)}, bf16[6,128,256]{2,1,0:T(8,128)(2,1)S(1)}, u32[]{:S(2)}, u32[]{:S(2)}) collective-permute-start(bf16[6,128,256]{2,1,0:T(8,128)(2,1)S(1)} %collective-permute-done.rest_2_), channel_id=1, source_target_pairs={{0,4},{4,0},{8,12},{12,8},{16,20},{20,16},{24,28},{28,24},{1,5},{5... | collective-permute-start | bytes 1179656 | tf_op jit(solution)/shard_map/ppermute | solution.py:165
  27.2 26.6 %collective-permute-start.5 = (bf16[6,128,256]{2,1,0:T(8,128)(2,1)S(1)}, bf16[6,128,256]{2,1,0:T(8,128)(2,1)S(1)}, u32[]{:S(2)}, u32[]{:S(2)}) collective-permute-start(bf16[6,128,256]{2,1,0:T(8,128)(2,1)S(1)} %collective-permute-done.1.rest_4_), channel_id=1, source_target_pairs={{0,4},{4,0},{8,12},{12,8},{16,20},{20,16},{24,28},{28,24},{1,5},{5... | collective-permute-start | bytes 1179656 | tf_op jit(solution)/shard_map/ppermute | solution.py:165
  27.7 37.4 %collective-permute-start.7 = (bf16[6,128,256]{2,1,0:T(8,128)(2,1)S(1)}, bf16[6,128,256]{2,1,0:T(8,128)(2,1)S(1)}, u32[]{:S(2)}, u32[]{:S(2)}) collective-permute-start(bf16[6,128,256]{2,1,0:T(8,128)(2,1)S(1)} %collective-permute-done.1.rest_4_), channel_id=1, source_target_pairs={{0,8},{4,12},{8,0},{12,4},{16,24},{20,28},{24,16},{28,20},{1,9},{5... | collective-permute-start | bytes 1179656 | tf_op jit(solution)/shard_map/ppermute | solution.py:165
  28.2 36.9 %collective-permute-start.8 = (bf16[6,128,256]{2,1,0:T(8,128)(2,1)S(1)}, bf16[6,128,256]{2,1,0:T(8,128)(2,1)S(1)}, u32[]{:S(2)}, u32[]{:S(2)}) collective-permute-start(bf16[6,128,256]{2,1,0:T(8,128)(2,1)S(1)} %collective-permute-done.rest_2_), channel_id=1, source_target_pairs={{1,0},{2,1},{3,2},{5,4},{6,5},{7,6},{9,8},{10,9},{11,10},{13,12},{... | collective-permute-start | bytes 1179656 | tf_op jit(solution)/shard_map/ppermute | solution.py:175
  29.5 0.7 copy-start.2
  30.3 23.5 %collective-permute-start.6 = (bf16[6,128,256]{2,1,0:T(8,128)(2,1)S(1)}, bf16[6,128,256]{2,1,0:T(8,128)(2,1)S(1)}, u32[]{:S(2)}, u32[]{:S(2)}) collective-permute-start(bf16[6,128,256]{2,1,0:T(8,128)(2,1)S(1)} %collective-permute-done.2.rest_6_), channel_id=1, source_target_pairs={{0,4},{4,0},{8,12},{12,8},{16,20},{20,16},{24,28},{28,24},{1,5},{5... | collective-permute-start | bytes 1179656 | tf_op jit(solution)/shard_map/ppermute | solution.py:165
  30.3 23.5 %copy-start.3 = (bf16[6,128,256]{2,1,0:T(8,128)(2,1)S(1)}, bf16[6,128,256]{2,1,0:T(8,128)(2,1)}, u32[]{:S(2)}) copy-start(bf16[6,128,256]{2,1,0:T(8,128)(2,1)} %copy-done.2) | copy-start | bytes 1179652
  30.3 34.8 %collective-permute-start.9 = (bf16[6,128,256]{2,1,0:T(8,128)(2,1)S(1)}, bf16[6,128,256]{2,1,0:T(8,128)(2,1)S(1)}, u32[]{:S(2)}, u32[]{:S(2)}) collective-permute-start(bf16[6,128,256]{2,1,0:T(8,128)(2,1)S(1)} %collective-permute-done.2.rest_6_), channel_id=1, source_target_pairs={{0,16},{4,20},{8,24},{12,28},{16,0},{20,4},{24,8},{28,12},{1,17},{... | collective-permute-start | bytes 1179656 | tf_op jit(solution)/shard_map/ppermute | solution.py:165
  49.8 4.0 %copy-start = (bf16[317,128,128]{2,1,0:T(8,128)(2,1)}, bf16[317,128,128]{2,1,0:T(8,128)(2,1)S(1)}, u32[]{:S(2)}) copy-start(bf16[317,128,128]{2,1,0:T(8,128)(2,1)S(1)} %shard_map.93.t_ref) | copy-start | bytes 31162372
  65.1 16.0 %collective-permute-start.12 = (bf16[6,128,256]{2,1,0:T(8,128)(2,1)S(1)}, bf16[6,128,256]{2,1,0:T(8,128)(2,1)S(1)}, u32[]{:S(2)}, u32[]{:S(2)}) collective-permute-start(bf16[6,128,256]{2,1,0:T(8,128)(2,1)S(1)} %collective-permute-done.9.rest_2_), channel_id=1, source_target_pairs={{0,4},{4,0},{8,12},{12,8},{16,20},{20,16},{24,28},{28,24},{1,5},{5... | collective-permute-start | bytes 1179656 | tf_op jit(solution)/shard_map/ppermute | solution.py:165
  65.2 15.9 %collective-permute-start.10 = (bf16[6,128,256]{2,1,0:T(8,128)(2,1)S(1)}, bf16[6,128,256]{2,1,0:T(8,128)(2,1)S(1)}, u32[]{:S(2)}, u32[]{:S(2)}) collective-permute-start(bf16[6,128,256]{2,1,0:T(8,128)(2,1)S(1)} %collective-permute-done.7.rest_0_), channel_id=1, source_target_pairs={{0,4},{4,0},{8,12},{12,8},{16,20},{20,16},{24,28},{28,24},{1,5},{5... | collective-permute-start | bytes 1179656 | tf_op jit(solution)/shard_map/ppermute | solution.py:165
  65.8 15.3 %collective-permute-start.11 = (bf16[6,128,256]{2,1,0:T(8,128)(2,1)S(1)}, bf16[6,128,256]{2,1,0:T(8,128)(2,1)S(1)}, u32[]{:S(2)}, u32[]{:S(2)}) collective-permute-start(bf16[6,128,256]{2,1,0:T(8,128)(2,1)S(1)} %collective-permute-done.8.rest_1_), channel_id=1, source_target_pairs={{0,4},{4,0},{8,12},{12,8},{16,20},{20,16},{24,28},{28,24},{1,5},{5... | collective-permute-start | bytes 1179656 | tf_op jit(solution)/shard_map/ppermute | solution.py:165
  65.9 7.3 %collective-permute-start.13 = (bf16[3,128,256]{2,1,0:T(8,128)(2,1)S(1)}, bf16[3,128,256]{2,1,0:T(8,128)(2,1)S(1)}, u32[]{:S(2)}, u32[]{:S(2)}) collective-permute-start(bf16[3,128,256]{2,1,0:T(8,128)(2,1)S(1)} %slice.6), channel_id=1, source_target_pairs={{0,8},{4,12},{8,0},{12,4},{16,24},{20,28},{24,16},{28,20},{1,9},{5... | collective-permute-start | bytes 589832 | tf_op jit(solution)/shard_map/ppermute | solution.py:165
  66.8 6.7 %collective-permute-start.14 = (bf16[3,128,256]{2,1,0:T(8,128)(2,1)S(1)}, bf16[3,128,256]{2,1,0:T(8,128)(2,1)S(1)}, u32[]{:S(2)}, u32[]{:S(2)}) collective-permute-start(bf16[3,128,256]{2,1,0:T(8,128)(2,1)S(1)} %slice.7), channel_id=1, source_target_pairs={{0,16},{4,20},{8,24},{12,28},{16,0},{20,4},{24,8},{28,12},{1,17},{... | collective-permute-start | bytes 589832 | tf_op jit(solution)/shard_map/ppermute | solution.py:165
  73.1 8.0 %collective-permute-start.15 = (bf16[3,128,256]{2,1,0:T(8,128)(2,1)S(1)}, bf16[3,128,256]{2,1,0:T(8,128)(2,1)S(1)}, u32[]{:S(2)}, u32[]{:S(2)}) collective-permute-start(bf16[3,128,256]{2,1,0:T(8,128)(2,1)S(1)} %collective-permute-done.13.rest_3_), channel_id=1, source_target_pairs={{0,4},{4,0},{8,12},{12,8},{16,20},{20,16},{24,28},{28,24},{1,5},{5... | collective-permute-start | bytes 589832 | tf_op jit(solution)/shard_map/ppermute | solution.py:165
  73.5 7.6 %collective-permute-start.16 = (bf16[3,128,256]{2,1,0:T(8,128)(2,1)S(1)}, bf16[3,128,256]{2,1,0:T(8,128)(2,1)S(1)}, u32[]{:S(2)}, u32[]{:S(2)}) collective-permute-start(bf16[3,128,256]{2,1,0:T(8,128)(2,1)S(1)} %collective-permute-done.14.rest_4_), channel_id=1, source_target_pairs={{0,4},{4,0},{8,12},{12,8},{16,20},{20,16},{24,28},{28,24},{1,5},{5... | collective-permute-start | bytes 589832 | tf_op jit(solution)/shard_map/ppermute | solution.py:165
